TPU v7x, 1024 devices: a whole 8x8x8 slice. The times are simulated.
1024 devices in a mesh: section: 16 (over x_hi, y), tp: 8 (over z), dp: 8 (over x_lo, core).
Axes of the slice: x: 8 (x_hi: 2, x_lo: 4; x = x_hi * 4 + x_lo), y: 8, z: 8, core: 2. Of those that a mesh axis runs over, the one named last changes fastest.
Arguments:
- stash: bfloat16 [16, 8, 320, 48, 384], P('section', 'dp', None, 'tp'), may hold values from -24 to 24
- grad_out: bfloat16 [16, 8, 320, 6144], P('section', 'dp', None, 'tp'), may hold values from -6 to 6
- doc_lengths: int32 [16, 8, 8], P('section', 'dp'), may hold values from 1 to 160, 320 in all within a row
Outputs:
- qkv_grad: bfloat16 [16, 8, 320, 48, 384], P('section', 'dp', None, 'tp')
- bias_grad: float32 [16, 48, 384], P('section', 'tp')
Inputs may be any that keep to these rules, and one draw needn't show every extreme that they name: `doc_lengths`: the 8 lengths of one micro-batch sum to 320, and in each micro-batch one of them is exactly 160.
All inputs are finite; a program needn't handle non-finite values.
Results may differ from a plain program's by a relative error of at most 0.012.
Values may be sent and summed in bfloat16 or wider, within the bound.
A program may use at most 32 MiB of HBM per device.

v0:
```python
import math

import jax
import jax.numpy as jnp
from jax import lax
from jax.sharding import PartitionSpec as P


def sent_to_all(value, axis):
    copies = jnp.broadcast_to(value, (lax.axis_size(axis), *value.shape))
    return lax.all_to_all(copies, axis, split_axis=0, concat_axis=0, tiled=True)


def of_everyone(value, axis):
    return sent_to_all(value, axis).sum(axis=0)


def segment_of(lengths, row_count):
    doc_ends = jnp.cumsum(lengths)
    position = jnp.arange(row_count, dtype=jnp.int32)
    return jnp.sum((position[:, None] >= doc_ends[None, :]).astype(jnp.int32), axis=1)


def attention_grads(packed, grad_rows, lengths):
    row_count, head_count, pack_width = packed.shape
    head_size = pack_width // 3
    inv_root = 1.0 / math.sqrt(head_size)
    queries = packed[:, :, :head_size]
    keys_in = packed[:, :, head_size : 2 * head_size]
    values_in = packed[:, :, 2 * head_size :]
    grad_heads = grad_rows.reshape(row_count, head_count, head_size)
    segment = segment_of(lengths, row_count)
    position = jnp.arange(row_count, dtype=jnp.int32)
    allowed = (segment[:, None] == segment[None, :]) & (position[None, :] <= position[:, None])
    scores = (
        jnp.einsum("qhd,khd->hqk", queries, keys_in, preferred_element_type=jnp.float32) * inv_root
    )
    masked = jnp.where(allowed[None], scores, -jnp.inf)
    row_top = jnp.max(masked, axis=-1, keepdims=True)
    raised = jnp.exp(masked - row_top)
    attn_prob = raised / jnp.sum(raised, axis=-1, keepdims=True)
    prob_low = attn_prob.astype(jnp.bfloat16)
    attn_out = jnp.einsum("hqk,khd->qhd", prob_low, values_in, preferred_element_type=jnp.float32)
    row_dot = jnp.einsum("qhd,qhd->hq", grad_heads.astype(jnp.float32), attn_out)
    prob_grad = jnp.einsum(
        "qhd,khd->hqk", grad_heads, values_in, preferred_element_type=jnp.float32
    )
    score_grad = attn_prob * (prob_grad - row_dot[:, :, None]) * inv_root
    score_low = score_grad.astype(jnp.bfloat16)
    query_grad = jnp.einsum("hqk,khd->qhd", score_low, keys_in, preferred_element_type=jnp.float32)
    key_grad = jnp.einsum("hqk,qhd->khd", score_low, queries, preferred_element_type=jnp.float32)
    value_grad = jnp.einsum(
        "hqk,qhd->khd", prob_low, grad_heads, preferred_element_type=jnp.float32
    )
    return jnp.concatenate([query_grad, key_grad, value_grad], axis=-1)


def send_back(received):
    return lax.all_to_all(jnp.flip(received, 0), "section", split_axis=0, concat_axis=0, tiled=True)


def mirror_fetch(stash):
    packed = stash[0, 0]
    row_count, head_count, pack_width = packed.shape
    section_count = lax.axis_size("section")
    blocks = packed.reshape(section_count, row_count // section_count, head_count, pack_width)
    returned = send_back(lax.all_to_all(blocks, "section", split_axis=0, concat_axis=0, tiled=True))
    return returned.reshape(row_count, head_count, pack_width)


def body(stash, grad_out, doc_lengths):
    fetched = mirror_fetch(stash)
    grads = attention_grads(fetched, grad_out[0, 0], doc_lengths[0, 0])
    qkv_grad = grads.astype(jnp.bfloat16)[None, None]
    bias_local = jnp.sum(grads, axis=0)
    bias_total = of_everyone(bias_local, "dp")
    bias_grad = (bias_total / lax.axis_size("dp"))[None]
    return (qkv_grad, bias_grad)


def solution(mesh):
    in_specs = (
        P("section", "dp", None, "tp", None),
        P("section", "dp", None, "tp"),
        P("section", "dp", None),
    )
    out_specs = (P("section", "dp", None, "tp", None), P("section", "tp", None))
    return jax.shard_map(body, mesh=mesh, in_specs=in_specs, out_specs=out_specs, check_vma=False)
```

profile of v0, /device:TPU:113, one launch (start us, length us, event | category | flops | bytes accessed | tf_op | source)
XLA Modules:
  0.0 137.1 jit_solution(13188681884240475660)
XLA Ops:
  0.6 2.3 %reshape_squeeze.6 = bf16[16,20,6,384]{3,1,0,2:T(8,128)(2,1)S(1)} reshape(bf16[1,1,320,6,384]{4,2,3,1,0:T(8,128)(2,1)} %param.3) | data formatting | bytes 2949120 | tf_op jit(solution)/shard_map/reshape;squeeze | solution.py:66
  2.9 0.2 copy.31
  3.1 45.2 %all_to_all.15 = bf16[16,20,6,384]{3,1,2,0:T(8,128)(2,1)S(1)} all-to-all(bf16[16,20,6,384]{3,1,2,0:T(8,128)(2,1)S(1)} %copy.31), channel_id=1, replica_groups=mesh['section'=16,'tp'=8,'dp'=8] {'section'}, dimensions={0} | all-to-all | bytes 2949120 | tf_op jit(solution)/shard_map/all_to_all | solution.py:67
  48.3 1.4 %rev.4 = bf16[16,20,6,384]{3,1,2,0:T(8,128)(2,1)} reverse(bf16[16,20,6,384]{3,1,2,0:T(8,128)(2,1)S(1)} %all_to_all.15), dimensions={0} | reverse | bytes 2949120 | tf_op jit(solution)/shard_map/jit(_flip)/rev | solution.py:59
  49.7 16.5 %all-to-all-start.1 = ((bf16[16,20,6,384]{3,1,2,0:T(8,128)(2,1)}), bf16[16,20,6,384]{3,1,2,0:T(8,128)(2,1)S(1)}, u32[]{:S(2)}, u32[]{:S(2)}) async-start(bf16[16,20,6,384]{3,1,2,0:T(8,128)(2,1)} %rev.4), calls=%async_computation.1 | async-start | bytes 3538944 | tf_op jit(solution)/shard_map/all_to_all | solution.py:59
  66.2 0.0 copy-done
  66.2 1.1 copy.33
  67.3 1.1 copy.52
  68.4 0.2 reduce-window.8
  68.5 0.1 convert_reduce_fusion
  68.6 0.8 fusion.7
  69.4 37.7 %all-to-all-done.1 = bf16[16,20,6,384]{3,1,2,0:T(8,128)(2,1)S(1)} async-done(((bf16[16,20,6,384]{3,1,2,0:T(8,128)(2,1)}), bf16[16,20,6,384]{3,1,2,0:T(8,128)(2,1)S(1)}, u32[]{:S(2)}, u32[]{:S(2)}) %all-to-all-start.1) | async-done | bytes 1474592 | tf_op jit(solution)/shard_map/all_to_all | solution.py:59
  107.1 0.2 copy.32
  107.3 0.0 copy-start.3
  107.3 0.4 reshape.131
  107.7 0.5 fusion.11
  108.3 0.0 copy-start.1
  108.3 1.1 fusion.19
  109.4 0.6 convolution_bitcast_fusion
  109.9 0.5 copy-done.2
  110.4 0.7 fusion.5
  111.1 0.7 multiply_convert_fusion
  111.8 0.5 convolution_bitcast_fusion.1
  112.3 0.7 convolution_bitcast_fusion.2
  113.0 0.1 convert_bitcast_fusion.2
  113.0 0.1 convert_bitcast_fusion
  113.2 0.1 maximum_reduce_fusion
  113.4 0.6 broadcast_in_dim.16
  114.0 17.0 %all-to-all-start.2 = ((f32[8,6,384]{2,1,0:T(8,128)}), f32[8,6,384]{2,1,0:T(8,128)S(1)}, u32[]{:S(2)}, u32[]{:S(2)}) async-start(f32[8,6,384]{2,1,0:T(8,128)} %broadcast_in_dim.16), calls=%async_computation.2 | async-start | bytes 196608 | tf_op jit(solution)/shard_map/all_to_all | solution.py:11
  131.0 1.3 pad_maximum_fusion
  132.3 4.2 %all-to-all-done.2 = f32[8,6,384]{2,1,0:T(8,128)S(1)} async-done(((f32[8,6,384]{2,1,0:T(8,128)}), f32[8,6,384]{2,1,0:T(8,128)S(1)}, u32[]{:S(2)}, u32[]{:S(2)}) %all-to-all-start.2) | async-done | bytes 73760 | tf_op jit(solution)/shard_map/all_to_all | solution.py:11
  136.5 0.6 copy.40
  (8 shorter events, 0.0 us)
Async XLA Ops:
  48.3 17.9 %copy-start = (bf16[1,1,320,768]{3,2,1,0:T(8,128)(2,1)S(1)}, bf16[1,1,320,768]{3,2,1,0:T(8,128)(2,1)}, u32[]{:S(2)}) copy-start(bf16[1,1,320,768]{3,2,1,0:T(8,128)(2,1)} %param.4) | copy-start | bytes 1474564
  49.7 18.7 %copy-start.4 = (s32[1,1,8]{2,1,0:T(1,128)S(1)}, s32[1,1,8]{2,1,0:T(1,128)}, u32[]{:S(2)}) copy-start(s32[1,1,8]{2,1,0:T(1,128)} %param.5) | copy-start | bytes 100
  49.7 57.4 %all-to-all-start.1 = ((bf16[16,20,6,384]{3,1,2,0:T(8,128)(2,1)}), bf16[16,20,6,384]{3,1,2,0:T(8,128)(2,1)S(1)}, u32[]{:S(2)}, u32[]{:S(2)}) async-start(bf16[16,20,6,384]{3,1,2,0:T(8,128)(2,1)} %rev.4), calls=%async_computation.1 | async-start | bytes 3538944 | tf_op jit(solution)/shard_map/all_to_all | solution.py:59
  107.3 0.9 copy-start.3
  108.3 1.1 copy-start.1
  109.3 1.1 copy-start.2
  114.0 22.5 %all-to-all-start.2 = ((f32[8,6,384]{2,1,0:T(8,128)}), f32[8,6,384]{2,1,0:T(8,128)S(1)}, u32[]{:S(2)}, u32[]{:S(2)}) async-start(f32[8,6,384]{2,1,0:T(8,128)} %broadcast_in_dim.16), calls=%async_computation.2 | async-start | bytes 196608 | tf_op jit(solution)/shard_map/all_to_all | solution.py:11
where the time goes:
time: 139 us; the launch traced here: 137 us
  blocking collectives  45.2 us (33%)
  waiting for transfers between devices  41.9 us (30%)
  starting transfers between devices  33.6 us (24%)
  local copies, waits for them, and re-layouts  8.32 us (6%)
  other arithmetic  3.78 us (3%)
  matrix products  3.62 us (3%)
    all_to_all x1, blocking collectives, mirror_fetch(): lax.all_to_all(blocks, 'section', split_axis=0, concat_axis=0, tiled=True)  45.2 us
    all_to_all x1, waiting for transfers between devices, send_back(): lax.all_to_all(jnp.flip(received, 0), 'section', split_axis=0, concat_axi...  37.7 us
    all_to_all x1, starting transfers between devices, sent_to_all(): return lax.all_to_all(copies, axis, split_axis=0, concat_axis=0, tiled=True)  17 us
    all_to_all x1, starting transfers between devices, send_back(): lax.all_to_all(jnp.flip(received, 0), 'section', split_axis=0, concat_axi...  16.5 us
    all_to_all x1, waiting for transfers between devices, sent_to_all(): return lax.all_to_all(copies, axis, split_axis=0, concat_axis=0, tiled=True)  4.17 us
    unnamed x13, local copies, waits for them, and re-layouts  3.25 us
  transfers between devices with their start and end apart: 2, of which 2 were waited for; matrix products, arithmetic and copies ran while one was open for 3% of the time, Pallas kernels for 0%

commit v1 on v0

v1 whole, which is shorter than its diff:
```python
import functools
import math

import jax
import jax.numpy as jnp
from jax import lax
from jax.experimental import pallas as pl
from jax.experimental.pallas import tpu as pltpu
from jax.sharding import PartitionSpec as P

MESH = pl.DeviceIdType.MESH
CUTS = 4


def partners(sections, x_parts, y_parts):
    section = lax.axis_index("section")
    x_hi, y = section // y_parts, section % y_parts
    over = (1 - x_hi) * y_parts + y
    flipped = x_hi * y_parts + (y_parts - 1 - y)
    return over, flipped


def allowed_bias(ends_ref, docs, rows):
    query = lax.broadcasted_iota(jnp.int32, (1, rows), 1)
    start = jnp.zeros((1, rows), jnp.int32)
    end = jnp.int32(0)
    for d in range(docs):
        end = end + ends_ref[d]
        start = jnp.where(query >= end, end, start)
    key = lax.broadcasted_iota(jnp.int32, (rows, rows), 0)
    query = lax.broadcasted_iota(jnp.int32, (rows, rows), 1)
    return jnp.where((key <= query) & (key >= start), 0.0, -jnp.inf).astype(jnp.float32)


def head_grads(q, k, v, g, mask):
    inv_root = 1.0 / math.sqrt(q.shape[-1])
    nt = (((1,), (1,)), ((), ()))
    tn = (((0,), (0,)), ((), ()))
    nn = (((1,), (0,)), ((), ()))
    dot = functools.partial(lax.dot_general, preferred_element_type=jnp.float32)
    scores = dot(k, q, nt) * (inv_root * math.log2(math.e)) + mask
    raised = jnp.exp2(scores - jnp.max(scores, axis=0, keepdims=True))
    prob = raised * (1.0 / jnp.sum(raised, axis=0, keepdims=True))
    prob_low = prob.astype(jnp.bfloat16)
    prob_grad = dot(v, g, nt)
    row_dot = jnp.sum(prob_low.astype(jnp.float32) * prob_grad, axis=0, keepdims=True)
    score_low = (prob * (prob_grad - row_dot) * inv_root).astype(jnp.bfloat16)
    return dot(score_low, k, tn), dot(score_low, q, nn), dot(prob_low, g, nn)


def kernel(shape, stash, grad_out, lengths, made, bias_out, relay, land, g_all, mask, bias_part, bias_all,
           s1, r1, s2, r2, g_sem, bias_send, bias_recv):
    sections, x_parts, y_parts, replicas = shape
    heads, rows, width = land.shape
    size = width // 3
    cut = rows // CUTS
    over, flipped = partners(sections, x_parts, y_parts)
    me = lax.axis_index("dp")
    peers = [lax.rem(me + n, replicas) for n in range(1, replicas)]

    barrier = pltpu.get_barrier_semaphore()
    for to in (over, flipped):
        pl.semaphore_signal(barrier, inc=1, device_id={"section": to}, device_id_type=MESH)
    for to in peers:
        pl.semaphore_signal(barrier, inc=1, device_id={"dp": to}, device_id_type=MESH)
    g_copy = pltpu.make_async_copy(grad_out, g_all, g_sem)
    g_copy.start()
    pl.semaphore_wait(barrier, 2 + len(peers))

    def piece(ref, h, n):
        return ref.at[h, pl.ds(n * cut, cut)]

    def hop(src, dst, send, recv, h, n, to):
        at = h * CUTS + n
        return pltpu.make_async_remote_copy(
            src_ref=piece(src, h, n), dst_ref=piece(dst, h, n), send_sem=send.at[at],
            recv_sem=recv.at[at], device_id={"section": to}, device_id_type=MESH)

    def first(h, n):
        return hop(stash, relay, s1, r1, h, n, over if n % 2 else flipped)

    def second(h, n):
        return hop(relay, land, s2, r2, h, n, flipped if n % 2 else over)

    @pl.loop(0, heads)
    def _(h):
        for n in range(CUTS):
            first(h, n).start()

    mask[...] = allowed_bias(lengths, lengths.shape[0], rows)

    @pl.loop(0, heads)
    def _(h):
        for n in range(CUTS):
            first(h, n).wait_recv()
            second(h, n).start()

    g_copy.wait()

    @pl.loop(0, heads)
    def _(h):
        for n in range(CUTS):
            second(h, n).wait_recv()
        q = land[h, :, 0:size]
        k = land[h, :, size:2 * size]
        v = land[h, :, 2 * size:]
        g = g_all[:, pl.ds(pl.multiple_of(h * size, size), size)]
        for n, part in enumerate(head_grads(q, k, v, g, mask[...])):
            made[h, :, n * size:(n + 1) * size] = part.astype(made.dtype)
            bias_part[h, :, n * size:(n + 1) * size] = jnp.sum(part.reshape(-1, 8, size), axis=0)

    def bias_copy(n):
        return pltpu.make_async_remote_copy(
            src_ref=bias_all.at[me], dst_ref=bias_all.at[me], send_sem=bias_send.at[n],
            recv_sem=bias_recv.at[n], device_id={"dp": peers[n]}, device_id_type=MESH)

    for h in range(heads):
        bias_all[me, h:h + 1] = jnp.sum(bias_part[h], axis=0, keepdims=True)
    for n in range(len(peers)):
        bias_copy(n).start()

    @pl.loop(0, heads)
    def _(h):
        for n in range(CUTS):
            first(h, n).wait_send()
            second(h, n).wait_send()

    for n in range(len(peers)):
        bias_copy(n).wait()
    total = bias_all[0]
    for n in range(1, replicas):
        total = total + bias_all[n]
    total = total / replicas
    for h in range(heads):
        bias_out[h] = total[h:h + 1]


def solution(mesh):
    sections, replicas = mesh.shape["section"], mesh.shape["dp"]
    x_parts = 2
    shape = (sections, x_parts, sections // x_parts, replicas)

    def body(stash, grad_out, doc_lengths):
        _, _, rows, heads, width = stash.shape
        held = jnp.transpose(stash[0, 0], (1, 0, 2))
        pieces = heads * CUTS
        dma = pltpu.SemaphoreType.DMA
        made, bias = pl.pallas_call(
            functools.partial(kernel, shape),
            out_shape=(jax.ShapeDtypeStruct(held.shape, held.dtype),
                       jax.ShapeDtypeStruct((heads, 1, width), jnp.float32)),
            in_specs=[pl.BlockSpec(memory_space=pltpu.HBM), pl.BlockSpec(memory_space=pltpu.HBM),
                      pl.BlockSpec(memory_space=pltpu.SMEM)],
            out_specs=(pl.BlockSpec(memory_space=pltpu.VMEM), pl.BlockSpec(memory_space=pltpu.VMEM)),
            scratch_shapes=[
                pltpu.VMEM(held.shape, held.dtype),
                pltpu.VMEM(held.shape, held.dtype),
                pltpu.VMEM(grad_out.shape[2:], grad_out.dtype),
                pltpu.VMEM((rows, rows), jnp.float32),
                pltpu.VMEM((heads, 8, width), jnp.float32),
                pltpu.VMEM((replicas, heads, width), jnp.float32),
                dma((pieces,)), dma((pieces,)), dma((pieces,)), dma((pieces,)),
                dma, dma((replicas - 1,)), dma((replicas - 1,)),
            ],
            compiler_params=pltpu.CompilerParams(
                collective_id=0, has_side_effects=True, vmem_limit_bytes=40 << 20),
            name="mirror_attention_grads",
        )(held, grad_out[0, 0], doc_lengths[0, 0])
        return jnp.transpose(made, (1, 0, 2))[None, None], jnp.transpose(bias, (1, 0, 2))

    in_specs = (
        P("section", "dp", None, "tp", None),
        P("section", "dp", None, "tp"),
        P("section", "dp", None),
    )
    out_specs = (P("section", "dp", None, "tp", None), P("section", "tp", None))
    return jax.shard_map(body, mesh=mesh, in_specs=in_specs, out_specs=out_specs, check_vma=False)
```

time: 139 us -> 95.6 us (0.69)
  the two profiles are of different devices: /device:TPU:113 before, /device:TPU:15 now
where the time goes in v1:
time: 95.6 us; the launch traced here: 95.4 us
  Pallas kernels  90 us (94%)
  local copies, waits for them, and re-layouts  4.76 us (5%)
    pallas_call x1, Pallas kernels, body(): pl.pallas_call(functools.partial(kernel, shape), out_shape=(jax.ShapeDtyp...  90 us
    unnamed x8, local copies, waits for them, and re-layouts  4.76 us

profile of v1, /device:TPU:15, one launch (start us, length us, event | category | flops | bytes accessed | tf_op | source)
XLA Modules:
  0.0 95.4 jit_solution(5793993634142399207)
XLA Ops:
  0.6 0.0 copy-start
  0.6 1.4 %copy-done = bf16[1,1,320,6,384]{4,2,3,1,0:T(8,128)(2,1)S(1)} copy-done((bf16[1,1,320,6,384]{4,2,3,1,0:T(8,128)(2,1)S(1)}, bf16[1,1,320,6,384]{4,2,3,1,0:T(8,128)(2,1)}, u32[]{:S(2)}) %copy-start) | copy-done | bytes 1474584
  2.0 0.0 copy-start.1
  2.0 1.0 %copy-done.1 = bf16[1,1,320,768]{3,2,1,0:T(8,128)(2,1)S(1)} copy-done((bf16[1,1,320,768]{3,2,1,0:T(8,128)(2,1)S(1)}, bf16[1,1,320,768]{3,2,1,0:T(8,128)(2,1)}, u32[]{:S(2)}) %copy-start.1) | copy-done | bytes 491544
  3.0 0.0 copy-start.2
  3.0 0.7 copy-done.2
  3.7 90.0 %mirror_attention_grads.1 = (bf16[6,320,384]{2,1,0:T(8,128)(2,1)S(1)}, f32[6,1,384]{2,1,0:T(1,128)S(1)}) custom-call(bf16[6,320,384]{2,1,0:T(8,128)(2,1)S(1)} %bitcast.9, bf16[320,768]{1,0:T(8,128)(2,1)S(1)} %bitcast.11, s32[8]{0:T(128)S(1)} %bitcast.13), custom_call_target="tpu_custom_call" | custom-call | tf_op jit(solution)/shard_map/mirror_attention_grads/pallas_call | solution.py:148
  93.7 1.1 %copy.7 = bf16[1,1,320,6,384]{4,2,3,1,0:T(8,128)(2,1)} copy(bf16[1,1,320,6,384]{4,2,3,1,0:T(8,128)(2,1)S(1)} %bitcast.10) | data formatting | bytes 2949120
  94.8 0.6 copy.8
Async XLA Ops:
  0.6 1.4 %copy-start = (bf16[1,1,320,6,384]{4,2,3,1,0:T(8,128)(2,1)S(1)}, bf16[1,1,320,6,384]{4,2,3,1,0:T(8,128)(2,1)}, u32[]{:S(2)}) copy-start(bf16[1,1,320,6,384]{4,2,3,1,0:T(8,128)(2,1)} %param.3) | copy-start | bytes 4423684
  2.0 1.0 %copy-start.1 = (bf16[1,1,320,768]{3,2,1,0:T(8,128)(2,1)S(1)}, bf16[1,1,320,768]{3,2,1,0:T(8,128)(2,1)}, u32[]{:S(2)}) copy-start(bf16[1,1,320,768]{3,2,1,0:T(8,128)(2,1)} %param.4) | copy-start | bytes 1474564
  3.0 0.7 copy-start.2

commit v2 on v1

--- a/solution.py
+++ b/solution.py
@@ -10,6 +10,7 @@
 
 MESH = pl.DeviceIdType.MESH
 CUTS = 4
+LIMIT = 56 << 20
 
 
 def partners(sections, x_parts, y_parts):
@@ -48,24 +49,31 @@
     return dot(score_low, k, tn), dot(score_low, q, nn), dot(prob_low, g, nn)
 
 
-def kernel(shape, stash, grad_out, lengths, made, bias_out, relay, land, g_all, mask, bias_part, bias_all,
-           s1, r1, s2, r2, g_sem, bias_send, bias_recv):
-    sections, x_parts, y_parts, replicas = shape
+def exchange_kernel(shape, stash, grad_out, lengths, out, bias_local, own, relay, land, made, g_all, mask,
+                    bias_part, s1, r1, s2, r2, own_sem, out_sem, g_sem):
+    sections, x_parts, y_parts = shape
     heads, rows, width = land.shape
     size = width // 3
     cut = rows // CUTS
     over, flipped = partners(sections, x_parts, y_parts)
-    me = lax.axis_index("dp")
-    peers = [lax.rem(me + n, replicas) for n in range(1, replicas)]
 
     barrier = pltpu.get_barrier_semaphore()
     for to in (over, flipped):
         pl.semaphore_signal(barrier, inc=1, device_id={"section": to}, device_id_type=MESH)
-    for to in peers:
-        pl.semaphore_signal(barrier, inc=1, device_id={"dp": to}, device_id_type=MESH)
+
+    def load(h):
+        return pltpu.make_async_copy(stash.at[h], own.at[h], own_sem.at[h])
+
+    def store(h):
+        return pltpu.make_async_copy(made.at[h], out.at[h], out_sem.at[h])
+
+    @pl.loop(0, heads)
+    def _(h):
+        load(h).start()
+
     g_copy = pltpu.make_async_copy(grad_out, g_all, g_sem)
     g_copy.start()
-    pl.semaphore_wait(barrier, 2 + len(peers))
+    pl.semaphore_wait(barrier, 2)
 
     def piece(ref, h, n):
         return ref.at[h, pl.ds(n * cut, cut)]
@@ -77,13 +85,14 @@
             recv_sem=recv.at[at], device_id={"section": to}, device_id_type=MESH)
 
     def first(h, n):
-        return hop(stash, relay, s1, r1, h, n, over if n % 2 else flipped)
+        return hop(own, relay, s1, r1, h, n, over if n % 2 else flipped)
 
     def second(h, n):
         return hop(relay, land, s2, r2, h, n, flipped if n % 2 else over)
 
     @pl.loop(0, heads)
     def _(h):
+        load(h).wait()
         for n in range(CUTS):
             first(h, n).start()
 
@@ -108,25 +117,39 @@
         for n, part in enumerate(head_grads(q, k, v, g, mask[...])):
             made[h, :, n * size:(n + 1) * size] = part.astype(made.dtype)
             bias_part[h, :, n * size:(n + 1) * size] = jnp.sum(part.reshape(-1, 8, size), axis=0)
-
-    def bias_copy(n):
-        return pltpu.make_async_remote_copy(
-            src_ref=bias_all.at[me], dst_ref=bias_all.at[me], send_sem=bias_send.at[n],
-            recv_sem=bias_recv.at[n], device_id={"dp": peers[n]}, device_id_type=MESH)
+        store(h).start()
 
     for h in range(heads):
-        bias_all[me, h:h + 1] = jnp.sum(bias_part[h], axis=0, keepdims=True)
-    for n in range(len(peers)):
-        bias_copy(n).start()
+        bias_local[h:h + 1] = jnp.sum(bias_part[h], axis=0, keepdims=True)
 
     @pl.loop(0, heads)
     def _(h):
         for n in range(CUTS):
             first(h, n).wait_send()
             second(h, n).wait_send()
-
-    for n in range(len(peers)):
-        bias_copy(n).wait()
+        store(h).wait()
+
+
+def bias_kernel(replicas, bias_local, bias_out, bias_all, bias_send, bias_recv, own_sem):
+    heads = bias_local.shape[0]
+    me = lax.axis_index("dp")
+    peers = [lax.rem(me + n, replicas) for n in range(1, replicas)]
+    barrier = pltpu.get_barrier_semaphore()
+    for to in peers:
+        pl.semaphore_signal(barrier, inc=1, device_id={"dp": to}, device_id_type=MESH)
+    own = pltpu.make_async_copy(bias_local, bias_all.at[me], own_sem)
+    own.start()
+    pl.semaphore_wait(barrier, len(peers))
+    copies = [
+        pltpu.make_async_remote_copy(
+            src_ref=bias_local, dst_ref=bias_all.at[me], send_sem=bias_send.at[n],
+            recv_sem=bias_recv.at[n], device_id={"dp": to}, device_id_type=MESH)
+        for n, to in enumerate(peers)
+    ]
+    for copy in copies:
+        copy.start()
+    for copy in [own, *copies]:
+        copy.wait()
     total = bias_all[0]
     for n in range(1, replicas):
         total = total + bias_all[n]
@@ -138,34 +161,47 @@
 def solution(mesh):
     sections, replicas = mesh.shape["section"], mesh.shape["dp"]
     x_parts = 2
-    shape = (sections, x_parts, sections // x_parts, replicas)
+    shape = (sections, x_parts, sections // x_parts)
+    vmem, hbm = pl.BlockSpec(memory_space=pltpu.VMEM), pl.BlockSpec(memory_space=pltpu.HBM)
 
     def body(stash, grad_out, doc_lengths):
         _, _, rows, heads, width = stash.shape
         held = jnp.transpose(stash[0, 0], (1, 0, 2))
         pieces = heads * CUTS
         dma = pltpu.SemaphoreType.DMA
-        made, bias = pl.pallas_call(
-            functools.partial(kernel, shape),
+        made, bias_local = pl.pallas_call(
+            functools.partial(exchange_kernel, shape),
             out_shape=(jax.ShapeDtypeStruct(held.shape, held.dtype),
-                       jax.ShapeDtypeStruct((heads, 1, width), jnp.float32)),
-            in_specs=[pl.BlockSpec(memory_space=pltpu.HBM), pl.BlockSpec(memory_space=pltpu.HBM),
-                      pl.BlockSpec(memory_space=pltpu.SMEM)],
-            out_specs=(pl.BlockSpec(memory_space=pltpu.VMEM), pl.BlockSpec(memory_space=pltpu.VMEM)),
+                       jax.ShapeDtypeStruct((heads, width), jnp.float32)),
+            in_specs=[hbm, hbm, pl.BlockSpec(memory_space=pltpu.SMEM)],
+            out_specs=(hbm, vmem),
             scratch_shapes=[
+                pltpu.VMEM(held.shape, held.dtype),
+                pltpu.VMEM(held.shape, held.dtype),
                 pltpu.VMEM(held.shape, held.dtype),
                 pltpu.VMEM(held.shape, held.dtype),
                 pltpu.VMEM(grad_out.shape[2:], grad_out.dtype),
                 pltpu.VMEM((rows, rows), jnp.float32),
                 pltpu.VMEM((heads, 8, width), jnp.float32),
-                pltpu.VMEM((replicas, heads, width), jnp.float32),
                 dma((pieces,)), dma((pieces,)), dma((pieces,)), dma((pieces,)),
-                dma, dma((replicas - 1,)), dma((replicas - 1,)),
+                dma((heads,)), dma((heads,)), dma,
             ],
             compiler_params=pltpu.CompilerParams(
-                collective_id=0, has_side_effects=True, vmem_limit_bytes=40 << 20),
+                collective_id=0, has_side_effects=True, vmem_limit_bytes=LIMIT),
             name="mirror_attention_grads",
         )(held, grad_out[0, 0], doc_lengths[0, 0])
+        bias = pl.pallas_call(
+            functools.partial(bias_kernel, replicas),
+            out_shape=jax.ShapeDtypeStruct((heads, 1, width), jnp.float32),
+            in_specs=[hbm],
+            out_specs=vmem,
+            scratch_shapes=[
+                pltpu.VMEM((replicas, heads, width), jnp.float32),
+                dma((replicas - 1,)), dma((replicas - 1,)), dma,
+            ],
+            compiler_params=pltpu.CompilerParams(collective_id=1, has_side_effects=True),
+            name="bias_mean",
+        )(bias_local)
         return jnp.transpose(made, (1, 0, 2))[None, None], jnp.transpose(bias, (1, 0, 2))
 
     in_specs = (

time: 95.6 us -> 124 us (1.30)
  the two profiles are of different devices: /device:TPU:15 before, /device:TPU:655 now
where the time goes in v2:
time: 124 us
  Pallas kernels  120 us (97%)
  local copies, waits for them, and re-layouts  3.24 us (3%)
    pallas_call x1, Pallas kernels, body(): pl.pallas_call(functools.partial(exchange_kernel, shape), out_shape=(jax....  106 us
    pallas_call x1, Pallas kernels, body(): pl.pallas_call(functools.partial(bias_kernel, replicas), out_shape=jax.Sh...  13.4 us
    unnamed x4, local copies, waits for them, and re-layouts  3.24 us

profile of v2, /device:TPU:655, one launch (start us, length us, event | category | flops | bytes accessed | tf_op | source)
XLA Modules:
  0.0 123.5 jit_solution(5770580301177712687)
XLA Ops:
  0.6 106.2 %mirror_attention_grads.1 = (bf16[6,320,384]{2,1,0:T(8,128)(2,1)}, f32[6,384]{1,0:T(8,128)}) custom-call(bf16[6,320,384]{2,1,0:T(8,128)(2,1)} %bitcast.9, bf16[320,768]{1,0:T(8,128)(2,1)} %bitcast.11, s32[8]{0:T(128)} %bitcast.13), custom_call_target="tpu_custom_call" | custom-call | tf_op jit(solution)/shard_map/mirror_attention_grads/pallas_call | solution.py:172
  106.9 13.4 %bias_mean.1 = f32[6,1,384]{2,1,0:T(1,128)} custom-call(f32[6,384]{1,0:T(8,128)} %get-tuple-element.5.bias_local), custom_call_target="tpu_custom_call" | custom-call | tf_op jit(solution)/shard_map/bias_mean/pallas_call | solution.py:193
  120.3 0.0 copy-start
  120.3 2.6 %copy.7 = bf16[1,1,320,6,384]{4,2,3,1,0:T(8,128)(2,1)} copy(bf16[1,1,320,6,384]{4,2,3,1,0:T(8,128)(2,1)} %bitcast.10) | data formatting | bytes 2949120
  122.9 0.0 copy-done
  122.9 0.6 copy.8
Async XLA Ops:
  120.3 2.6 %copy-start = (f32[6,1,384]{2,1,0:T(1,128)S(1)}, f32[6,1,384]{2,1,0:T(1,128)}, u32[]{:S(2)}) copy-start(f32[6,1,384]{2,1,0:T(1,128)} %bias_mean.1) | copy-start | bytes 27652

commit v3 on v1

--- a/solution.py
+++ b/solution.py
@@ -10,6 +10,8 @@
 
 MESH = pl.DeviceIdType.MESH
 CUTS = 4
+SHIFT = 1
+LIMIT = 52 << 20
 
 
 def partners(sections, x_parts, y_parts):
@@ -48,8 +50,8 @@
     return dot(score_low, k, tn), dot(score_low, q, nn), dot(prob_low, g, nn)
 
 
-def kernel(shape, stash, grad_out, lengths, made, bias_out, relay, land, g_all, mask, bias_part, bias_all,
-           s1, r1, s2, r2, g_sem, bias_send, bias_recv):
+def kernel(shape, stash, grad_out, lengths, made, bias_out, own, from_over, from_flipped, land, g_all, mask,
+           bias_part, bias_all, s1, r_over, r_flipped, s_over, s_flipped, r2, own_sem, g_sem, bias_send, bias_recv):
     sections, x_parts, y_parts, replicas = shape
     heads, rows, width = land.shape
     size = width // 3
@@ -58,49 +60,110 @@
     me = lax.axis_index("dp")
     peers = [lax.rem(me + n, replicas) for n in range(1, replicas)]
 
+    def load(h):
+        return pltpu.make_async_copy(stash.at[h], own.at[h], own_sem.at[h])
+
     barrier = pltpu.get_barrier_semaphore()
-    for to in (over, flipped):
-        pl.semaphore_signal(barrier, inc=1, device_id={"section": to}, device_id_type=MESH)
+
+    def greet(**to):
+        pl.semaphore_signal(barrier, inc=1, device_id=to, device_id_type=MESH)
+
+    greet(section=over)
+    greet(section=flipped)
+
     for to in peers:
-        pl.semaphore_signal(barrier, inc=1, device_id={"dp": to}, device_id_type=MESH)
+        greet(dp=to)
+
+    @pl.loop(0, heads)
+    def _(h):
+        load(h).start()
+
     g_copy = pltpu.make_async_copy(grad_out, g_all, g_sem)
     g_copy.start()
     pl.semaphore_wait(barrier, 2 + len(peers))
 
-    def piece(ref, h, n):
-        return ref.at[h, pl.ds(n * cut, cut)]
-
     def hop(src, dst, send, recv, h, n, to):
-        at = h * CUTS + n
+        at, rows_at = h * CUTS + n, pl.ds(n * cut, cut)
         return pltpu.make_async_remote_copy(
-            src_ref=piece(src, h, n), dst_ref=piece(dst, h, n), send_sem=send.at[at],
+            src_ref=src.at[h, rows_at], dst_ref=dst.at[h, rows_at], send_sem=send.at[at],
             recv_sem=recv.at[at], device_id={"section": to}, device_id_type=MESH)
 
-    def first(h, n):
-        return hop(stash, relay, s1, r1, h, n, over if n % 2 else flipped)
-
-    def second(h, n):
-        return hop(relay, land, s2, r2, h, n, flipped if n % 2 else over)
-
-    @pl.loop(0, heads)
-    def _(h):
-        for n in range(CUTS):
-            first(h, n).start()
+    def x_first(h, n):
+        return hop(own, from_over, s1, r_over, h, n, over)
+
+    def y_first(h, n):
+        return hop(own, from_flipped, s1, r_flipped, h, n, flipped)
+
+    def y_second(h, n):
+        return hop(from_over, land, s_over, r2, h, n, flipped)
+
+    def x_second(h, n):
+        return hop(from_flipped, land, s_flipped, r2, h, n, over)
+
+    y = lax.axis_index("section") % y_parts
+    first_plane = lax.axis_index("tp") == 0
+    low = first_plane & (y == 0)
+    high = first_plane & (y == y_parts - 1)
+
+    def goes_x_first(h, n, low, high):
+        moved = h < SHIFT
+        if n == 1:
+            return jnp.logical_not(low & moved)
+        return high & moved if n == 0 else jnp.bool_(n % 2)
+
+    def each(h, n, sent, passed):
+        if n > 1:
+            if n % 2:
+                sent(x_first, h, n)
+                passed(x_first, y_second, h, n)
+            else:
+                sent(y_first, h, n)
+                passed(y_first, x_second, h, n)
+            return
+        mine = goes_x_first(h, n, low, high)
+
+        @pl.when(mine)
+        def _():
+            sent(x_first, h, n)
+            passed(x_first, y_second, h, n)
+
+        @pl.when(jnp.logical_not(mine))
+        def _():
+            sent(y_first, h, n)
+
+        @pl.when(jnp.logical_not(goes_x_first(h, n, high, low)))
+        def _():
+            passed(y_first, x_second, h, n)
+
+    def nothing(*_):
+        pass
+
+    def start(away, h, n):
+        away(h, n).start()
+
+    def forward(arrived, onward, h, n):
+        arrived(h, n).wait_recv()
+        onward(h, n).start()
+
+    @pl.loop(0, heads)
+    def _(h):
+        load(h).wait()
+        for n in range(CUTS):
+            each(h, n, start, nothing)
 
     mask[...] = allowed_bias(lengths, lengths.shape[0], rows)
 
     @pl.loop(0, heads)
     def _(h):
         for n in range(CUTS):
-            first(h, n).wait_recv()
-            second(h, n).start()
+            each(h, n, nothing, forward)
 
     g_copy.wait()
 
     @pl.loop(0, heads)
     def _(h):
         for n in range(CUTS):
-            second(h, n).wait_recv()
+            x_second(h, n).wait_recv()
         q = land[h, :, 0:size]
         k = land[h, :, size:2 * size]
         v = land[h, :, 2 * size:]
@@ -116,14 +179,20 @@
 
     for h in range(heads):
         bias_all[me, h:h + 1] = jnp.sum(bias_part[h], axis=0, keepdims=True)
+
+    def sent_wait(away, h, n):
+        away(h, n).wait_send()
+
+    def passed_wait(arrived, onward, h, n):
+        onward(h, n).wait_send()
+
     for n in range(len(peers)):
         bias_copy(n).start()
 
     @pl.loop(0, heads)
     def _(h):
         for n in range(CUTS):
-            first(h, n).wait_send()
-            second(h, n).wait_send()
+            each(h, n, sent_wait, passed_wait)
 
     for n in range(len(peers)):
         bias_copy(n).wait()
@@ -155,15 +224,17 @@
             scratch_shapes=[
                 pltpu.VMEM(held.shape, held.dtype),
                 pltpu.VMEM(held.shape, held.dtype),
+                pltpu.VMEM(held.shape, held.dtype),
+                pltpu.VMEM(held.shape, held.dtype),
                 pltpu.VMEM(grad_out.shape[2:], grad_out.dtype),
                 pltpu.VMEM((rows, rows), jnp.float32),
                 pltpu.VMEM((heads, 8, width), jnp.float32),
                 pltpu.VMEM((replicas, heads, width), jnp.float32),
-                dma((pieces,)), dma((pieces,)), dma((pieces,)), dma((pieces,)),
-                dma, dma((replicas - 1,)), dma((replicas - 1,)),
+                *[dma((pieces,))] * 6,
+                dma((heads,)), dma, dma((replicas - 1,)), dma((replicas - 1,)),
             ],
             compiler_params=pltpu.CompilerParams(
-                collective_id=0, has_side_effects=True, vmem_limit_bytes=40 << 20),
+                collective_id=0, has_side_effects=True, vmem_limit_bytes=LIMIT),
             name="mirror_attention_grads",
         )(held, grad_out[0, 0], doc_lengths[0, 0])
         return jnp.transpose(made, (1, 0, 2))[None, None], jnp.transpose(bias, (1, 0, 2))

time: 95.6 us -> 89.3 us (0.934)
  the two profiles are of different devices: /device:TPU:15 before, /device:TPU:113 now
where the time goes in v3:
time: 89.3 us; the launch traced here: 88.9 us
  Pallas kernels  84.8 us (95%)
  local copies, waits for them, and re-layouts  3.39 us (4%)
    pallas_call x1, Pallas kernels, body(): pl.pallas_call(functools.partial(kernel, shape), out_shape=(jax.ShapeDtyp...  84.8 us
    unnamed x6, local copies, waits for them, and re-layouts  3.39 us

profile of v3, /device:TPU:113, one launch (start us, length us, event | category | flops | bytes accessed | tf_op | source)
XLA Modules:
  0.0 88.9 jit_solution(11734079174229038577)
XLA Ops:
  0.6 0.0 copy-start
  0.6 1.0 %copy-done = bf16[1,1,320,768]{3,2,1,0:T(8,128)(2,1)S(1)} copy-done((bf16[1,1,320,768]{3,2,1,0:T(8,128)(2,1)S(1)}, bf16[1,1,320,768]{3,2,1,0:T(8,128)(2,1)}, u32[]{:S(2)}) %copy-start) | copy-done | bytes 491544
  1.7 0.0 copy-start.1
  1.7 0.7 copy-done.1
  2.3 84.8 %mirror_attention_grads.1 = (bf16[6,320,384]{2,1,0:T(8,128)(2,1)S(1)}, f32[6,1,384]{2,1,0:T(1,128)S(1)}) custom-call(bf16[6,320,384]{2,1,0:T(8,128)(2,1)} %bitcast.13, bf16[320,768]{1,0:T(8,128)(2,1)S(1)} %bitcast.10, s32[8]{0:T(128)S(1)} %bitcast.12), custom_call_target="tpu_custom_call" | custom-call | tf_op jit(solution)/shard_map/mirror_attention_grads/pallas_call | solution.py:217
  87.1 1.1 %copy.7 = bf16[1,1,320,6,384]{4,2,3,1,0:T(8,128)(2,1)} copy(bf16[1,1,320,6,384]{4,2,3,1,0:T(8,128)(2,1)S(1)} %bitcast.9) | data formatting | bytes 2949120
  88.3 0.6 copy.8
Async XLA Ops:
  0.6 1.0 %copy-start = (bf16[1,1,320,768]{3,2,1,0:T(8,128)(2,1)S(1)}, bf16[1,1,320,768]{3,2,1,0:T(8,128)(2,1)}, u32[]{:S(2)}) copy-start(bf16[1,1,320,768]{3,2,1,0:T(8,128)(2,1)} %param.4) | copy-start | bytes 1474564
  1.7 0.7 copy-start.1

commit v4 on v3

--- a/solution.py
+++ b/solution.py
@@ -51,7 +51,7 @@
 
 
 def kernel(shape, stash, grad_out, lengths, made, bias_out, own, from_over, from_flipped, land, g_all, mask,
-           bias_part, bias_all, s1, r_over, r_flipped, s_over, s_flipped, r2, own_sem, g_sem, bias_send, bias_recv):
+           bias_part, bias_all, s1, r_over, r_flipped, s_over, s_flipped, r2, own_sem, g_sem, bias_send, bias_recv, ends, ends_sem):
     sections, x_parts, y_parts, replicas = shape
     heads, rows, width = land.shape
     size = width // 3
@@ -80,6 +80,8 @@
 
     g_copy = pltpu.make_async_copy(grad_out, g_all, g_sem)
     g_copy.start()
+    ends_copy = pltpu.make_async_copy(lengths, ends, ends_sem)
+    ends_copy.start()
     pl.semaphore_wait(barrier, 2 + len(peers))
 
     def hop(src, dst, send, recv, h, n, to):
@@ -151,7 +153,8 @@
         for n in range(CUTS):
             each(h, n, start, nothing)
 
-    mask[...] = allowed_bias(lengths, lengths.shape[0], rows)
+    ends_copy.wait()
+    mask[...] = allowed_bias(ends, ends.shape[0], rows)
 
     @pl.loop(0, heads)
     def _(h):
@@ -218,8 +221,7 @@
             functools.partial(kernel, shape),
             out_shape=(jax.ShapeDtypeStruct(held.shape, held.dtype),
                        jax.ShapeDtypeStruct((heads, 1, width), jnp.float32)),
-            in_specs=[pl.BlockSpec(memory_space=pltpu.HBM), pl.BlockSpec(memory_space=pltpu.HBM),
-                      pl.BlockSpec(memory_space=pltpu.SMEM)],
+            in_specs=[pl.BlockSpec(memory_space=pltpu.HBM)] * 3,
             out_specs=(pl.BlockSpec(memory_space=pltpu.VMEM), pl.BlockSpec(memory_space=pltpu.VMEM)),
             scratch_shapes=[
                 pltpu.VMEM(held.shape, held.dtype),
@@ -232,11 +234,14 @@
                 pltpu.VMEM((replicas, heads, width), jnp.float32),
                 *[dma((pieces,))] * 6,
                 dma((heads,)), dma, dma((replicas - 1,)), dma((replicas - 1,)),
+                pltpu.SMEM(doc_lengths.shape[2:], doc_lengths.dtype), dma,
             ],
             compiler_params=pltpu.CompilerParams(
                 collective_id=0, has_side_effects=True, vmem_limit_bytes=LIMIT),
             name="mirror_attention_grads",
-        )(held, grad_out[0, 0], doc_lengths[0, 0])
+        )(pltpu.with_memory_space_constraint(held, pltpu.HBM),
+          pltpu.with_memory_space_constraint(grad_out[0, 0], pltpu.HBM),
+          pltpu.with_memory_space_constraint(doc_lengths[0, 0], pltpu.HBM))
         return jnp.transpose(made, (1, 0, 2))[None, None], jnp.transpose(bias, (1, 0, 2))
 
     in_specs = (

time: 89.3 us -> 87.2 us (0.976)
  local copies, waits for them, and re-layouts: 3.39 us -> 1.71 us
    unnamed x6 -> x2, local copies, waits for them, and re-layouts: 3.39 us -> 1.71 us
where the time goes in v4:
time: 87.2 us; the launch traced here: 86.6 us
  Pallas kernels  84.3 us (97%)
  local copies, waits for them, and re-layouts  1.71 us (2%)
    pallas_call x1, Pallas kernels, body(): pl.pallas_call(functools.partial(kernel, shape), out_shape=(jax.ShapeDtyp...  84.3 us

profile of v4, /device:TPU:113, one launch (start us, length us, event | category | flops | bytes accessed | tf_op | source)
XLA Modules:
  0.0 86.6 jit_solution(12027892658532505170)
XLA Ops:
  0.6 84.3 %mirror_attention_grads.1 = (bf16[6,320,384]{2,1,0:T(8,128)(2,1)S(1)}, f32[6,1,384]{2,1,0:T(1,128)S(1)}) custom-call(bf16[6,320,384]{2,1,0:T(8,128)(2,1)} %bitcast.11, bf16[320,768]{1,0:T(8,128)(2,1)} %bitcast.12, s32[8]{0:T(128)} %bitcast.13), custom_call_target="tpu_custom_call" | custom-call | tf_op jit(solution)/shard_map/mirror_attention_grads/pallas_call | solution.py:220
  84.9 1.1 %copy.7 = bf16[1,1,320,6,384]{4,2,3,1,0:T(8,128)(2,1)} copy(bf16[1,1,320,6,384]{4,2,3,1,0:T(8,128)(2,1)S(1)} %bitcast.9) | data formatting | bytes 2949120
  86.0 0.6 copy.8

commit v5 on v4

--- a/solution.py
+++ b/solution.py
@@ -9,7 +9,7 @@
 from jax.sharding import PartitionSpec as P
 
 MESH = pl.DeviceIdType.MESH
-CUTS = 4
+CUTS = 2
 SHIFT = 1
 LIMIT = 52 << 20
 
@@ -104,36 +104,26 @@
 
     y = lax.axis_index("section") % y_parts
     first_plane = lax.axis_index("tp") == 0
-    low = first_plane & (y == 0)
-    high = first_plane & (y == y_parts - 1)
-
-    def goes_x_first(h, n, low, high):
+    late = first_plane & (y == 0)
+    mirror = first_plane & (y == y_parts - 1)
+
+    def each(h, n, sent, passed):
+        if n % 2:
+            sent(x_first, h, n)
+            passed(x_first, y_second, h, n)
+            return
         moved = h < SHIFT
-        if n == 1:
-            return jnp.logical_not(low & moved)
-        return high & moved if n == 0 else jnp.bool_(n % 2)
-
-    def each(h, n, sent, passed):
-        if n > 1:
-            if n % 2:
-                sent(x_first, h, n)
-                passed(x_first, y_second, h, n)
-            else:
-                sent(y_first, h, n)
-                passed(y_first, x_second, h, n)
-            return
-        mine = goes_x_first(h, n, low, high)
-
-        @pl.when(mine)
+
+        @pl.when(mirror & moved)
         def _():
             sent(x_first, h, n)
             passed(x_first, y_second, h, n)
 
-        @pl.when(jnp.logical_not(mine))
+        @pl.when(jnp.logical_not(mirror & moved))
         def _():
             sent(y_first, h, n)
 
-        @pl.when(jnp.logical_not(goes_x_first(h, n, high, low)))
+        @pl.when(jnp.logical_not(late & moved))
         def _():
             passed(y_first, x_second, h, n)
 
@@ -205,6 +195,15 @@
     total = total / replicas
     for h in range(heads):
         bias_out[h] = total[h:h + 1]
+
+
+def write_kernel(made, bias, made_out, bias_out, made_sem, bias_sem):
+    copies = [pltpu.make_async_copy(bias, bias_out, bias_sem)]
+    copies += [pltpu.make_async_copy(made.at[h], made_out.at[h], made_sem.at[h]) for h in range(made.shape[0])]
+    for copy in copies:
+        copy.start()
+    for copy in copies:
+        copy.wait()
 
 
 def solution(mesh):
@@ -242,6 +241,16 @@
         )(pltpu.with_memory_space_constraint(held, pltpu.HBM),
           pltpu.with_memory_space_constraint(grad_out[0, 0], pltpu.HBM),
           pltpu.with_memory_space_constraint(doc_lengths[0, 0], pltpu.HBM))
+        made, bias = pl.pallas_call(
+            write_kernel,
+            out_shape=(jax.ShapeDtypeStruct(made.shape, made.dtype),
+                       jax.ShapeDtypeStruct(bias.shape, bias.dtype)),
+            in_specs=[pl.BlockSpec(memory_space=pltpu.VMEM)] * 2,
+            out_specs=(pl.BlockSpec(memory_space=pltpu.HBM),) * 2,
+            scratch_shapes=[dma((heads,)), dma],
+            name="write_results",
+        )(pltpu.with_memory_space_constraint(made, pltpu.VMEM),
+          pltpu.with_memory_space_constraint(bias, pltpu.VMEM))
         return jnp.transpose(made, (1, 0, 2))[None, None], jnp.transpose(bias, (1, 0, 2))
 
     in_specs = (

time: 87.2 us -> 86.5 us (level)
  local copies, waits for them, and re-layouts: 1.71 us -> 0 us
    unnamed x2 -> x0, local copies, waits for them, and re-layouts: 1.71 us -> none
    pallas_call x0 -> x1, Pallas kernels: none -> 1.17 us  [body(): pl.pallas_call(write_kernel, out_shape=(jax.ShapeDtypeStruct(made.shape,...]
where the time goes in v5:
time: 86.5 us; the launch traced here: 85.4 us
  Pallas kernels  84.7 us (98%)
    pallas_call x1, Pallas kernels, body(): pl.pallas_call(functools.partial(kernel, shape), out_shape=(jax.ShapeDtyp...  83.5 us

profile of v5, /device:TPU:113, one launch (start us, length us, event | category | flops | bytes accessed | tf_op | source)
XLA Modules:
  0.0 85.4 jit_solution(17351451260324950119)
XLA Ops:
  0.6 83.5 %mirror_attention_grads.1 = (bf16[6,320,384]{2,1,0:T(8,128)(2,1)S(1)}, f32[6,1,384]{2,1,0:T(1,128)S(1)}) custom-call(bf16[6,320,384]{2,1,0:T(8,128)(2,1)} %bitcast.9, bf16[320,768]{1,0:T(8,128)(2,1)} %bitcast.10, s32[8]{0:T(128)} %bitcast.11), custom_call_target="tpu_custom_call" | custom-call | tf_op jit(solution)/shard_map/mirror_attention_grads/pallas_call | solution.py:219
  84.2 1.2 %write_results.1 = (bf16[6,320,384]{2,1,0:T(8,128)(2,1)}, f32[6,1,384]{2,1,0:T(1,128)}) custom-call(bf16[6,320,384]{2,1,0:T(8,128)(2,1)S(1)} %get-tuple-element.6.made, f32[6,1,384]{2,1,0:T(1,128)S(1)} %get-tuple-element.7.bias), custom_call_target="tpu_custom_call" | custom-call | tf_op jit(solution)/shard_map/write_results/pallas_call | solution.py:244

commit v6 on v5

--- a/solution.py
+++ b/solution.py
@@ -108,11 +108,22 @@
     mirror = first_plane & (y == y_parts - 1)
 
     def each(h, n, sent, passed):
+        moved = (h < SHIFT) & (me % 2 == 1)
         if n % 2:
-            sent(x_first, h, n)
-            passed(x_first, y_second, h, n)
+            @pl.when(jnp.logical_not(late & moved))
+            def _():
+                sent(x_first, h, n)
+                passed(x_first, y_second, h, n)
+
+            @pl.when(late & moved)
+            def _():
+                sent(y_first, h, n)
+
+            @pl.when(mirror & moved)
+            def _():
+                passed(y_first, x_second, h, n)
+
             return
-        moved = h < SHIFT
 
         @pl.when(mirror & moved)
         def _():

time: 86.5 us -> 85.9 us (level); the launches traced: 85.4 us -> 85.7 us
  no operation moved by 1% of the time
where the time goes in v6:
time: 85.9 us; the launch traced here: 85.7 us
  Pallas kernels  85.1 us (99%)
    pallas_call x1, Pallas kernels, body(): pl.pallas_call(functools.partial(kernel, shape), out_shape=(jax.ShapeDtyp...  83.9 us

profile of v6, /device:TPU:113, one launch (start us, length us, event | category | flops | bytes accessed | tf_op | source)
XLA Modules:
  0.0 85.7 jit_solution(8239378660823165740)
XLA Ops:
  0.6 83.9 %mirror_attention_grads.1 = (bf16[6,320,384]{2,1,0:T(8,128)(2,1)S(1)}, f32[6,1,384]{2,1,0:T(1,128)S(1)}) custom-call(bf16[6,320,384]{2,1,0:T(8,128)(2,1)} %bitcast.9, bf16[320,768]{1,0:T(8,128)(2,1)} %bitcast.10, s32[8]{0:T(128)} %bitcast.11), custom_call_target="tpu_custom_call" | custom-call | tf_op jit(solution)/shard_map/mirror_attention_grads/pallas_call | solution.py:230
  84.5 1.2 %write_results.1 = (bf16[6,320,384]{2,1,0:T(8,128)(2,1)}, f32[6,1,384]{2,1,0:T(1,128)}) custom-call(bf16[6,320,384]{2,1,0:T(8,128)(2,1)S(1)} %get-tuple-element.6.made, f32[6,1,384]{2,1,0:T(1,128)S(1)} %get-tuple-element.7.bias), custom_call_target="tpu_custom_call" | custom-call | tf_op jit(solution)/shard_map/write_results/pallas_call | solution.py:255
